TPU v7x, 32 devices: a whole 2x2x4 slice. The times are simulated.
32 devices in a mesh: mem: 16 (over z, x, core), head: 2 (over y).
Axes of the slice: x: 2, y: 2, z: 4, core: 2. Of those that a mesh axis runs over, the one named last changes fastest.
Arguments:
- queries: bfloat16 [4096, 4096], P(('mem', 'head')), may hold values from -512 to 512
- local_keys: bfloat16 [4096, 1024], P(('mem', 'head')), may hold values from -6 to 6
- local_values: bfloat16 [4096, 1024], P(('mem', 'head')), may hold values from -12 to 12
- memory_keys: bfloat16 [65536, 1024], P('mem', 'head'), may hold values from -6 to 6
- memory_values: bfloat16 [65536, 1024], P('mem', 'head'), may hold values from -12 to 12
- block_ids: int32 [32, 8, 32], P('mem', 'head'), may hold values from 0 to 511, as said below
- mixing_offset_per_head: float32 [32], P('head'), may hold values from -2 to 2
Outputs:
- attended: bfloat16 [4096, 4096], P(('mem', 'head'))
Inputs may be any that keep to these rules, and one draw needn't show every extreme that they name: Each row block_ids[b, h] names 32 different blocks. Over the 2 query blocks of one index of mem and one key-value head, the named blocks with one value of n // 32 are at most 4 different ones; for some value exactly 4, each named by all 2 of those query blocks.
All inputs are finite; a program needn't handle non-finite values.
Results may differ from a plain program's by a relative error of at most 0.0033.
Values may be sent and summed in bfloat16 or wider, within the bound.
A program may use at most 128 MiB of HBM per device.

v0:
```python
import math

import jax
import jax.numpy as jnp
from jax import lax
from jax.sharding import PartitionSpec as P

HD = 128
QB = 128
BL = 128
TOPK = 32
WINDOW = 256


def from_behind(array, axis, by):
    count = lax.axis_size(axis)
    pairs = [(i, i + by) for i in range(count) if 0 <= i + by < count]
    return lax.ppermute(array, axis, pairs)


def attend_block(query_block, key_rows, value_rows, allowed):
    score_scale = 1.0 / math.sqrt(query_block.shape[-1])
    measure_grid_array = (
        jnp.einsum("tgd,kd->tgk", query_block, key_rows, preferred_element_type=jnp.float32)
        * score_scale
    )
    if allowed is not None:
        measure_grid_array = jnp.where(allowed[:, None, :], measure_grid_array, -1e30)
    highest = jnp.max(measure_grid_array, axis=2, keepdims=True)
    weights = jnp.exp(measure_grid_array - highest)
    denominator = jnp.sum(weights, axis=2, keepdims=True)
    mixed = jnp.einsum(
        "tgk,kd->tgd", weights.astype(jnp.bfloat16), value_rows, preferred_element_type=jnp.float32
    )
    return mixed / denominator


def plan_slots(block_ids, blocks_here, owner_count, capacity):
    block_rows, kv_local, top_count = block_ids.shape
    per_head = jnp.transpose(block_ids, (1, 0, 2)).reshape(kv_local, block_rows * top_count)
    owners = per_head // blocks_here
    within = per_head % blocks_here
    request_count = block_rows * top_count
    positions = jnp.arange(request_count, dtype=jnp.int32)
    earlier = positions[None, :] < positions[:, None]
    same_owner = owners[:, :, None] == owners[:, None, :]
    same_block = per_head[:, :, None] == per_head[:, None, :]
    leading = jnp.logical_not(jnp.any(same_block & earlier[None], axis=2))
    lead_rank = jnp.sum(same_owner & earlier[None] & leading[:, None, :], axis=2, dtype=jnp.int32)
    first_index = jnp.min(jnp.where(same_block, positions[None, None, :], request_count), axis=2)
    slot_rank = jnp.take_along_axis(lead_rank, first_index, axis=1)
    head_index = jnp.arange(kv_local, dtype=jnp.int32)[:, None]
    slot_index = (owners * kv_local + head_index) * capacity + slot_rank
    size_all = owner_count * kv_local * capacity
    target = jnp.where(leading, slot_index, size_all)
    slot_table = (
        jnp.full((size_all,), -1, jnp.int32)
        .at[target.reshape(-1)]
        .set(within.reshape(-1), mode="drop")
    )
    slot_table = slot_table.reshape(owner_count, kv_local, capacity)
    slot_index = jnp.transpose(slot_index.reshape(kv_local, block_rows, top_count), (1, 0, 2))
    return (slot_table, slot_index.reshape(block_rows * kv_local, top_count))


def fetch_blocks(slot_table, memory_keys, memory_values):
    kv_local = slot_table.shape[1]
    key_store = memory_keys.reshape(-1, BL, kv_local, HD)
    value_store = memory_values.reshape(-1, BL, kv_local, HD)
    safe_rows = jnp.maximum(
        lax.all_to_all(slot_table, "mem", split_axis=0, concat_axis=0, tiled=True), 0
    )
    head_index = jnp.arange(kv_local, dtype=jnp.int32)[None, :, None]
    key_blocks = key_store[safe_rows, :, head_index, :]
    value_blocks = value_store[safe_rows, :, head_index, :]
    return (
        lax.all_to_all(key_blocks, "mem", split_axis=0, concat_axis=0, tiled=True),
        lax.all_to_all(value_blocks, "mem", split_axis=0, concat_axis=0, tiled=True),
    )


def gather_memory(block_ids, memory_keys, memory_values):
    owner_count = lax.axis_size("mem")
    blocks_here = memory_keys.shape[0] // BL
    per_owner = (2 * TOPK + owner_count - 1) // owner_count
    slot_table, slot_index = plan_slots(block_ids, blocks_here, owner_count, per_owner)
    fetched_keys, fetched_values = fetch_blocks(slot_table, memory_keys, memory_values)
    return (fetched_keys.reshape(-1, BL, HD), fetched_values.reshape(-1, BL, HD), slot_index)


def per_device(
    queries, local_keys, local_values, memory_keys, memory_values, block_ids, mixing_offset_per_head
):
    q_heads, keys_own, values_own = (
        lax.all_to_all(queries, "head", split_axis=1, concat_axis=0, tiled=True),
        lax.all_to_all(local_keys, "head", split_axis=1, concat_axis=0, tiled=True),
        lax.all_to_all(local_values, "head", split_axis=1, concat_axis=0, tiled=True),
    )
    tokens_here = q_heads.shape[0]
    kv_local = keys_own.shape[1] // HD
    group_size = q_heads.shape[1] // (kv_local * HD)
    device_index = lax.axis_index("mem")
    block_rows = tokens_here // QB
    pair_count = block_rows * kv_local
    span = WINDOW + QB
    keys_before, earlier_values = from_behind((keys_own, values_own), "mem", 1)
    local_window_keys = jnp.concatenate([keys_before, keys_own], axis=0)
    window_values = jnp.concatenate([earlier_values, values_own], axis=0)
    gate_share = jax.nn.sigmoid(mixing_offset_per_head).reshape(kv_local, group_size)
    query_grid = q_heads.reshape(block_rows, QB, kv_local, group_size, HD)
    pair_list = jnp.arange(pair_count, dtype=jnp.int32)

    def query_of(couple_ordinal):
        block_index = couple_ordinal // kv_local
        head_local = couple_ordinal % kv_local
        zero = jnp.zeros((), jnp.int32)
        return lax.dynamic_slice(
            query_grid, (block_index, zero, head_local, zero, zero), (1, QB, 1, group_size, HD)
        ).reshape(QB, group_size, HD)

    def local_pair(couple_ordinal):
        block_index = couple_ordinal // kv_local
        head_local = couple_ordinal % kv_local
        start = tokens_here + block_index * QB - WINDOW
        key_rows = lax.dynamic_slice(local_window_keys, (start, head_local * HD), (span, HD))
        value_rows = lax.dynamic_slice(window_values, (start, head_local * HD), (span, HD))
        query_pos = device_index * tokens_here + block_index * QB + jnp.arange(QB, dtype=jnp.int32)
        key_pos = (
            device_index * tokens_here - tokens_here + start + jnp.arange(span, dtype=jnp.int32)
        )
        spacing_distance = query_pos[:, None] - key_pos[None, :]
        allowed = (key_pos[None, :] >= 0) & (spacing_distance >= 0) & (spacing_distance < WINDOW)
        return attend_block(query_of(couple_ordinal), key_rows, value_rows, allowed)

    def memory_pair(couple_ordinal, flat_keys, flat_values, slot_index):
        chosen = slot_index[couple_ordinal]
        key_rows = jnp.take(flat_keys, chosen, axis=0).reshape(-1, HD)
        value_rows = jnp.take(flat_values, chosen, axis=0).reshape(-1, HD)
        return attend_block(query_of(couple_ordinal), key_rows, value_rows, None)

    def blend(couple_ordinal, local_part, memory_part):
        share = gate_share[couple_ordinal % kv_local][None, :, None]
        return (share * memory_part + (1.0 - share) * local_part).astype(jnp.bfloat16)

    flat_keys, flat_values, slot_index = gather_memory(block_ids, memory_keys, memory_values)

    def both_parts(couple_ordinal):
        return blend(
            couple_ordinal,
            local_pair(couple_ordinal),
            memory_pair(couple_ordinal, flat_keys, flat_values, slot_index),
        )

    blended = lax.map(both_parts, pair_list)
    grid = blended.reshape(block_rows, kv_local, QB, group_size, HD)
    grid = jnp.transpose(grid, (0, 2, 1, 3, 4)).reshape(tokens_here, kv_local * group_size * HD)
    return lax.all_to_all(grid, "head", split_axis=0, concat_axis=1, tiled=True)


def solution(mesh):
    return jax.shard_map(
        per_device,
        mesh=mesh,
        in_specs=(
            P(("mem", "head"), None),
            P(("mem", "head"), None),
            P(("mem", "head"), None),
            P("mem", "head"),
            P("mem", "head"),
            P("mem", "head", None),
            P("head"),
        ),
        out_specs=P(("mem", "head"), None),
        check_vma=False,
    )
```

profile of v0, /device:TPU:16, one launch (start us, length us, event | category | flops | bytes accessed | tf_op | source)
XLA Modules:
  0.0 628.0 jit_solution(14877714742442868669)
XLA Ops:
  6.6 6.2 all-to-all-start.1
  22.1 4.0 all-to-all-done.4
  34.7 3.6 all-to-all-start
  38.3 6.9 %reshape.486 = bf16[32,128,4,128]{3,2,1,0:T(4,128)(2,1)} reshape(bf16[4096,512]{1,0:T(8,128)(2,1)} %param.14) | data formatting | bytes 8388608 | tf_op jit(solution)/shard_map/reshape | solution.py:68
  45.3 5.3 copy.58
  50.7 12.1 %gather_fusion.2 = bf16[256,128,128]{2,1,0:T(8,128)(2,1)} fusion(bf16[32,128,4,128]{3,1,2,0:T(8,128)(2,1)} %copy.58, s32[256]{0:T(256)S(1)} %reshape.443), kind=kCustom, calls=%fused_computation.2 | custom fusion | bytes 16779264 | tf_op jit(solution)/shard_map/gather | solution.py:74
  62.8 6.7 %all-to-all-start.2 = ((bf16[16,4,4,128,128]{4,3,2,1,0:T(8,128)(2,1)}), bf16[16,4,4,128,128]{4,3,2,1,0:T(8,128)(2,1)}, u32[]{:S(2)}, u32[]{:S(2)}) async-start(bf16[16,4,4,128,128]{4,3,2,1,0:T(8,128)(2,1)} %bitcast.109), calls=%async_computation.2 | async-start | bytes 16777216 | tf_op jit(solution)/shard_map/all_to_all | solution.py:77
  69.5 6.9 %reshape.487 = bf16[32,128,4,128]{3,2,1,0:T(4,128)(2,1)} reshape(bf16[4096,512]{1,0:T(8,128)(2,1)} %param.15) | data formatting | bytes 8388608 | tf_op jit(solution)/shard_map/reshape | solution.py:69
  76.4 5.3 copy.60
  81.7 12.1 %gather_fusion.3 = bf16[256,128,128]{2,1,0:T(8,128)(2,1)} fusion(bf16[32,128,4,128]{3,1,2,0:T(8,128)(2,1)} %copy.60, s32[256]{0:T(256)S(1)} %reshape.443), kind=kCustom, calls=%fused_computation.3 | custom fusion | bytes 16779264 | tf_op jit(solution)/shard_map/gather | solution.py:75
  93.8 158.2 %all-to-all-done.2 = bf16[16,4,4,128,128]{4,3,2,1,0:T(8,128)(2,1)} async-done(((bf16[16,4,4,128,128]{4,3,2,1,0:T(8,128)(2,1)}), bf16[16,4,4,128,128]{4,3,2,1,0:T(8,128)(2,1)}, u32[]{:S(2)}, u32[]{:S(2)}) %all-to-all-start.2) | async-done | bytes 8388640 | tf_op jit(solution)/shard_map/all_to_all | solution.py:77
  252.0 4.8 all-to-all-start.3
  259.1 3.5 collective-permute-start.1
  262.8 179.4 %collective-permute-done = bf16[256,512]{1,0:T(8,128)(2,1)S(1)} collective-permute-done((bf16[256,512]{1,0:T(8,128)(2,1)S(1)}, bf16[256,512]{1,0:T(8,128)(2,1)S(1)}, u32[]{:S(2)}, u32[]{:S(2)}) %collective-permute-start) | collective-permute-done | bytes 262176 | tf_op jit(solution)/shard_map/ppermute | solution.py:18
  445.8 164.9 %while.15 = (s32[]{:T(128)}, bf16[8,128,4,128]{3,1,2,0:T(8,128)(2,1)}, s32[8]{0:T(128)S(1)}, f32[4,4]{1,0:T(4,128)S(1)}, bf16[2,128,4,4,128]{1,4,3,2,0:T(8,128)(...) while((s32[]{:T(128)}, ...), condition=%wide.region_9.11_spmd, body=%wide.region_4.10_spmd.sunk | while | flops 1194246656 | bytes 39254676 | solution.py:154
  449.9 4.1 gather_fusion.1
  454.0 4.1 gather_fusion
  470.5 4.1 gather_fusion.1
  474.6 4.1 gather_fusion
  491.1 4.1 gather_fusion.1
  495.2 4.1 gather_fusion
  511.7 4.1 gather_fusion.1
  515.8 4.1 gather_fusion
  532.3 4.1 gather_fusion.1
  536.5 4.1 gather_fusion
  552.9 4.1 gather_fusion.1
  557.1 4.1 gather_fusion
  573.5 4.1 gather_fusion.1
  577.7 4.1 gather_fusion
  594.1 4.1 gather_fusion.1
  598.3 4.1 gather_fusion
  613.6 12.4 %all_to_all.88 = bf16[2,128,2048]{2,1,0:T(8,128)(2,1)S(1)} all-to-all(bf16[2,128,2048]{2,1,0:T(8,128)(2,1)S(1)} %all_to_all.77), channel_id=1, replica_groups=mesh['mem'=16,'head'=2] {'head'}, dimensions={0} | all-to-all | bytes 2097152 | tf_op jit(solution)/shard_map/all_to_all | solution.py:157
  (172 shorter events, 106.2 us)
Async XLA Ops:
  6.6 10.3 %all-to-all-start.1 = ((s32[16,4,4]{2,1,0:T(4,128)}), s32[16,4,4]{2,1,0:T(4,128)S(1)}, u32[]{:S(2)}, u32[]{:S(2)}) async-start(s32[16,4,4]{2,1,0:T(4,128)} %reshape.422), calls=%async_computation.1 | async-start | bytes 65536 | tf_op jit(solution)/shard_map/all_to_all | solution.py:71
  17.0 9.2 %all-to-all-start.4 = ((bf16[128,2,512]{2,0,1:T(8,128)(2,1)}), bf16[128,2,512]{2,0,1:T(8,128)(2,1)S(1)}, u32[]{:S(2)}, u32[]{:S(2)}) async-start(bf16[128,2,512]{2,0,1:T(8,128)(2,1)} %bitcast.85), calls=%async_computation.4 | async-start | bytes 524288 | tf_op jit(solution)/shard_map/all_to_all | solution.py:96
  26.1 8.6 %all-to-all-start.5 = ((bf16[128,2,512]{2,0,1:T(8,128)(2,1)}), bf16[128,2,512]{2,0,1:T(8,128)(2,1)S(1)}, u32[]{:S(2)}, u32[]{:S(2)}) async-start(bf16[128,2,512]{2,0,1:T(8,128)(2,1)} %bitcast.84), calls=%async_computation.5 | async-start | bytes 524288 | tf_op jit(solution)/shard_map/all_to_all | solution.py:97
  34.7 28.0 %all-to-all-start = ((bf16[128,2,2048]{0,2,1:T(8,128)(2,1)}), bf16[128,2,2048]{0,2,1:T(8,128)(2,1)S(1)}, u32[]{:S(2)}, u32[]{:S(2)}) async-start(bf16[128,2,2048]{0,2,1:T(8,128)(2,1)} %bitcast.11), calls=%async_computation | async-start | bytes 2097152 | tf_op jit(solution)/shard_map/all_to_all | solution.py:95
  62.8 189.2 %all-to-all-start.2 = ((bf16[16,4,4,128,128]{4,3,2,1,0:T(8,128)(2,1)}), bf16[16,4,4,128,128]{4,3,2,1,0:T(8,128)(2,1)}, u32[]{:S(2)}, u32[]{:S(2)}) async-start(bf16[16,4,4,128,128]{4,3,2,1,0:T(8,128)(2,1)} %bitcast.109), calls=%async_computation.2 | async-start | bytes 16777216 | tf_op jit(solution)/shard_map/all_to_all | solution.py:77
  252.0 7.0 %copy-start = (s32[2,4,32]{2,1,0:T(4,128)S(1)}, s32[2,4,32]{2,1,0:T(4,128)}, u32[]{:S(2)}) copy-start(s32[2,4,32]{2,1,0:T(4,128)} %param.16) | copy-start | bytes 3076
  252.0 10.6 %copy-start.1 = (f32[16]{0:T(128)S(1)}, f32[16]{0:T(128)}, u32[]{:S(2)}) copy-start(f32[16]{0:T(128)} %param.17) | copy-start | bytes 196
  252.0 193.8 %all-to-all-start.3 = ((bf16[16,4,4,128,128]{4,3,2,1,0:T(8,128)(2,1)}), bf16[16,4,4,128,128]{4,3,2,1,0:T(8,128)(2,1)}, u32[]{:S(2)}, u32[]{:S(2)}) async-start(bf16[16,4,4,128,128]{4,3,2,1,0:T(8,128)(2,1)} %bitcast.108), calls=%async_computation.3 | async-start | bytes 16777216 | tf_op jit(solution)/shard_map/all_to_all | solution.py:78
  257.0 185.1 %collective-permute-start = (bf16[256,512]{1,0:T(8,128)(2,1)S(1)}, bf16[256,512]{1,0:T(8,128)(2,1)S(1)}, u32[]{:S(2)}, u32[]{:S(2)}) collective-permute-start(bf16[256,512]{1,0:T(8,128)(2,1)S(1)} %bitcast.115), channel_id=1, source_target_pairs={{0,2},{2,4},{4,6},{6,8},{8,10},{10,12},{12,14},{14,16},{16,18},{18... | collective-permute-start | bytes 786440 | tf_op jit(solution)/shard_map/ppermute | solution.py:18
  259.1 185.8 %collective-permute-start.1 = (bf16[256,512]{1,0:T(8,128)(2,1)S(1)}, bf16[256,512]{1,0:T(8,128)(2,1)S(1)}, u32[]{:S(2)}, u32[]{:S(2)}) collective-permute-start(bf16[256,512]{1,0:T(8,128)(2,1)S(1)} %bitcast.117), channel_id=1, source_target_pairs={{0,2},{2,4},{4,6},{6,8},{8,10},{10,12},{12,14},{14,16},{16,18},{18... | collective-permute-start | bytes 786440 | tf_op jit(solution)/shard_map/ppermute | solution.py:18
where the time goes:
time: 631 us; the launch traced here: 628 us
  waiting for transfers between devices  349 us (55%)
  local copies, waits for them, and re-layouts  136 us (22%)
  matrix products  48.2 us (8%)
  starting transfers between devices  33.7 us (5%)
  loops' own time  28.1 us (4%)
  other arithmetic  20.4 us (3%)
  blocking collectives  12.4 us (2%)
    ppermute x2, waiting for transfers between devices, from_behind(): return lax.ppermute(array, axis, pairs)  181 us
    all_to_all x1, waiting for transfers between devices, fetch_blocks(): lax.all_to_all(key_blocks, 'mem', split_axis=0, concat_axis=0, tiled=True)  158 us
    gather x8, local copies, waits for them, and re-layouts, memory_pair(): value_rows = jnp.take(flat_values, chosen, axis=0).reshape(-1, HD)  33 us
    gather x8, local copies, waits for them, and re-layouts, memory_pair(): key_rows = jnp.take(flat_keys, chosen, axis=0).reshape(-1, HD)  33 us
    another operation x1, loops' own time, per_device(): blended = lax.map(both_parts, pair_list)  28.1 us
    dot_general x16, matrix products, attend_block(): jnp.einsum('tgk,kd->tgd', weights.astype(jnp.bfloat16), value_rows, prefe...  26.8 us
    dot_general x16, matrix products, attend_block(): jnp.einsum('tgd,kd->tgk', query_block, key_rows, preferred_element_type=j...  21.4 us
    reduce_sum x16, other arithmetic, attend_block(): denominator = jnp.sum(weights, axis=2, keepdims=True)  14.5 us
  transfers between devices with their start and end apart: 8, of which 6 were waited for; matrix products, arithmetic and copies ran while one was open for 9% of the time, Pallas kernels for 0%

commit v1 on v0

v1 whole, which is shorter than its diff:
```python
import functools
import math

import jax
import jax.numpy as jnp
from jax import lax
from jax.experimental import pallas as pl
from jax.experimental.pallas import tpu as pltpu
from jax.sharding import PartitionSpec as P

HD = 128
QB = 128
BL = 128
TOPK = 32
WINDOW = 256
LANES = 128
NONE = -1e30
SCALE2 = math.log2(math.e) / math.sqrt(HD)
VMEM_LIMIT = 56 * 1024 * 1024


def dot_t(a, b):
    return lax.dot_general(a, b, (((1,), (1,)), ((), ())), preferred_element_type=jnp.float32)


def lane_of(shape):
    return lax.broadcasted_iota(jnp.int32, shape, 1)


def split3(x):
    hi = x.astype(jnp.bfloat16).astype(jnp.float32)
    rest = x - hi
    mid = rest.astype(jnp.bfloat16).astype(jnp.float32)
    return hi, mid, rest - mid


def softmax_part(scores, values_and_ones):
    top = jnp.max(scores, axis=1, keepdims=True)
    weights = jnp.exp2((scores - top) * SCALE2).astype(jnp.bfloat16)
    both = jnp.dot(weights, values_and_ones, preferred_element_type=jnp.float32)
    return both[:, :HD], both[:, HD:], top


def part_kernel(group, half_heads, rows_per_chunk, cap, kv, sel, cnt, slots, q_ref, k_ref, v_ref, o_ref):
    chunk = 2 * pl.program_id(0) + sel[0]
    head = pl.program_id(1)
    col = pl.ds(pl.multiple_of(head * HD, HD), HD)
    width = (half_heads + 1) * HD

    @pl.when(head == 0)
    def _():
        for half in range(2):
            o_ref[0, :, half * width + half_heads * HD:(half + 1) * width] = jnp.zeros(
                (o_ref.shape[1], HD), jnp.bfloat16
            )

    def one_block(b, carry):
        pair = (chunk * rows_per_chunk + b) * kv + head
        rows = pl.ds(pl.multiple_of(b * QB, QB), QB)
        count = cnt[pair]

        def put(g, out, level):
            flat = head * group + g
            half = flat // half_heads
            at = flat - half * half_heads
            place = pl.multiple_of((flat + half) * HD, HD)
            o_ref[0, rows, pl.ds(place, HD)] = out.astype(jnp.bfloat16)
            stat = pl.ds(pl.multiple_of(half * width + half_heads * HD, HD), HD)
            lane = lane_of((QB, LANES))
            hi, mid, low = split3(level)
            old = o_ref[0, rows, stat].astype(jnp.float32)
            new = jnp.where(lane == at, hi, old)
            new = jnp.where(lane == at + 32, mid, new)
            new = jnp.where(lane == at + 64, low, new)
            o_ref[0, rows, stat] = new.astype(jnp.bfloat16)

        @pl.when(count == 0)
        def _():
            for g in range(group):
                put(g, jnp.zeros((QB, HD), jnp.float32), jnp.full((QB, LANES), NONE, jnp.float32))

        for size in range(1, cap + 1):
            @pl.when(count == size)
            def _(size=size):
                places = [
                    pl.ds(pl.multiple_of(slots[pair * cap + i] * BL, BL), BL) for i in range(size)
                ]
                keys = jnp.concatenate([k_ref[p, col] for p in places], axis=0)
                values = jnp.concatenate([v_ref[p, col] for p in places], axis=0)
                values = jnp.concatenate([values, jnp.ones_like(values)], axis=1)
                for g in range(group):
                    scores = dot_t(q_ref[rows, g * HD:(g + 1) * HD], keys)
                    out, total, top = softmax_part(scores, values)
                    put(g, out / total, top * SCALE2 + jnp.log2(total))

        return carry

    lax.fori_loop(0, rows_per_chunk, one_block, 0)


def memory_parts(sel, cnt, slots, queries, keys, values, chips, tokens, kv, group, cap):
    half_heads = kv * group // 2
    full = 2 * (half_heads + 1) * HD
    work = chips * tokens * kv * group * cap * BL // 2
    return pl.pallas_call(
        functools.partial(part_kernel, group, half_heads, tokens // QB, cap, kv),
        out_shape=jax.ShapeDtypeStruct((chips, tokens, full), jnp.bfloat16),
        grid_spec=pltpu.PrefetchScalarGridSpec(
            num_scalar_prefetch=3,
            grid=(chips, kv),
            in_specs=[
                pl.BlockSpec((tokens, group * HD), lambda c, h, s, n, t: (2 * c + s[0], h)),
                pl.BlockSpec(keys.shape, lambda c, h, s, n, t: (0, 0)),
                pl.BlockSpec(values.shape, lambda c, h, s, n, t: (0, 0)),
            ],
            out_specs=pl.BlockSpec((1, tokens, full), lambda c, h, s, n, t: (c, 0, 0)),
        ),
        compiler_params=pltpu.CompilerParams(vmem_limit_bytes=VMEM_LIMIT),
        cost_estimate=pl.CostEstimate(
            flops=work * HD * 6, bytes_accessed=chips * tokens * full * 4, transcendentals=work
        ),
        name="memory_parts",
    )(sel, cnt, slots, queries, keys, values)


def local_kernel(group, tokens, me, q_ref, k_ref, v_ref, o_ref):
    span = WINDOW + QB
    for b in range(tokens // QB):
        start = tokens + b * QB - WINDOW
        keys = k_ref[start:start + span, :]
        values = v_ref[start:start + span, :]
        values = jnp.concatenate([values, jnp.ones_like(values)], axis=1)
        rows = slice(b * QB, (b + 1) * QB)
        q_at = b * QB + lax.broadcasted_iota(jnp.int32, (QB, span), 0)
        k_at = start - tokens + lax.broadcasted_iota(jnp.int32, (QB, span), 1)
        gap = q_at - k_at
        allowed = (k_at + me[0] * tokens >= 0) & (gap >= 0) & (gap < WINDOW)
        for g in range(group):
            scores = dot_t(q_ref[rows, g * HD:(g + 1) * HD], keys)
            out, total, _ = softmax_part(jnp.where(allowed, scores, NONE), values)
            o_ref[rows, g * HD:(g + 1) * HD] = out / total


def local_part(me, queries, keys, values, kv, group):
    tokens = queries.shape[0]
    return pl.pallas_call(
        functools.partial(local_kernel, group, tokens),
        out_shape=jax.ShapeDtypeStruct(queries.shape, jnp.float32),
        grid_spec=pltpu.PrefetchScalarGridSpec(
            num_scalar_prefetch=1,
            grid=(kv,),
            in_specs=[
                pl.BlockSpec((tokens, group * HD), lambda h, m: (0, h)),
                pl.BlockSpec((keys.shape[0], HD), lambda h, m: (0, h)),
                pl.BlockSpec((keys.shape[0], HD), lambda h, m: (0, h)),
            ],
            out_specs=pl.BlockSpec((tokens, group * HD), lambda h, m: (0, h)),
        ),
        compiler_params=pltpu.CompilerParams(vmem_limit_bytes=VMEM_LIMIT),
        cost_estimate=pl.CostEstimate(
            flops=tokens * kv * group * 384 * HD * 6,
            bytes_accessed=tokens * kv * group * HD * 6,
            transcendentals=tokens * kv * group * 384,
        ),
        name="local_part",
    )(me, queries, keys, values)


def level_of(tile):
    x = tile.astype(jnp.float32)
    return x + pltpu.roll(x, LANES - 32, 1) + pltpu.roll(x, LANES - 64, 1)


def merge_half(half_heads, parts):
    levels = [level_of(part[:, half_heads * HD:]) for part in parts]
    top = functools.reduce(jnp.maximum, levels)
    weights = [jnp.exp2(level - top) for level in levels]
    total = functools.reduce(jnp.add, weights)
    shares = [w / total for w in weights]
    outs = []
    for at in range(half_heads):
        cols = slice(at * HD, (at + 1) * HD)
        outs.append(
            functools.reduce(
                jnp.add,
                [
                    part[:, cols].astype(jnp.float32) * share[:, at:at + 1]
                    for part, share in zip(parts, shares)
                ],
            )
        )
    return outs, top + jnp.log2(total)


def merge_kernel(half_heads, with_received, places, *refs):
    count = 6 if with_received else 4
    ins, outs = refs[:count], refs[count:]
    for half in range(2):
        parts = [ins[half][0], ins[2 + half][0]]
        if with_received:
            parts.append(ins[4 + half][...])
        merged, level = merge_half(half_heads, parts)
        for at, out in enumerate(merged):
            outs[half][:, at * HD:(at + 1) * HD] = out.astype(jnp.bfloat16)
        lane = lane_of(level.shape)
        hi, mid, low = split3(level)
        stat = jnp.where(lane < 32, hi, 0.0)
        stat = jnp.where((lane >= 32) & (lane < 64), pltpu.roll(mid, 32, 1), stat)
        stat = jnp.where((lane >= 64) & (lane < 96), pltpu.roll(low, 64, 1), stat)
        outs[half][:, half_heads * HD:] = stat.astype(jnp.bfloat16)


def final_kernel(half_heads, places, *refs):
    ins, local_ref, gate_ref, o_ref = refs[:6], refs[6], refs[7], refs[8]
    for half in range(2):
        parts = [ins[half][0], ins[2 + half][0], ins[4 + half][...]]
        merged, _ = merge_half(half_heads, parts)
        for at, out in enumerate(merged):
            flat = half * half_heads + at
            cols = slice(flat * HD, (flat + 1) * HD)
            share = gate_ref[:, cols]
            o_ref[:, cols] = (share * out + (1.0 - share) * local_ref[:, cols]).astype(jnp.bfloat16)


def merge_step(places, own, sib, received, half_heads, local=None, gate=None):
    tokens = own.shape[1]
    width = (half_heads + 1) * HD
    rows = QB // 2
    part_specs = [
        pl.BlockSpec((1, rows, width), lambda r, p: (p[0], r, 0)),
        pl.BlockSpec((1, rows, width), lambda r, p: (p[1], r, 1)),
    ]
    flat_spec = pl.BlockSpec((rows, width), lambda r, p: (r, 0))
    in_specs = part_specs * 2
    operands = [own, own, sib, sib]
    if received is not None:
        in_specs = in_specs + [flat_spec] * 2
        operands += list(received)
    if local is None:
        kernel = functools.partial(merge_kernel, half_heads, received is not None)
        out_shape = [jax.ShapeDtypeStruct((tokens, width), jnp.bfloat16)] * 2
        out_specs = [flat_spec] * 2
    else:
        kernel = functools.partial(final_kernel, half_heads)
        full = 2 * half_heads * HD
        wide = pl.BlockSpec((rows, full), lambda r, p: (r, 0))
        in_specs = in_specs + [wide, pl.BlockSpec((1, full), lambda r, p: (0, 0))]
        operands += [local, gate]
        out_shape = jax.ShapeDtypeStruct((tokens, full), jnp.bfloat16)
        out_specs = wide
    return pl.pallas_call(
        kernel,
        out_shape=out_shape,
        grid_spec=pltpu.PrefetchScalarGridSpec(
            num_scalar_prefetch=1, grid=(tokens // rows,), in_specs=in_specs, out_specs=out_specs
        ),
        compiler_params=pltpu.CompilerParams(vmem_limit_bytes=VMEM_LIMIT),
        name="merge_step" if local is None else "merge_last",
    )(places, *operands)


def chip_ring(chips):
    across = 1
    while across * 2 * across * 2 <= chips:
        across *= 2
    deep = chips // across
    walk = []
    for z in range(deep):
        row = range(1, across) if z % 2 == 0 else range(across - 1, 0, -1)
        walk += [z * across + x for x in row]
    return walk + [z * across for z in range(deep - 1, -1, -1)]


def block_tables(block_ids, first, blocks_here, cap):
    local = block_ids - first
    mine = (local >= 0) & (local < blocks_here)
    rank = jnp.cumsum(mine.astype(jnp.int32), axis=-1) - 1
    slots = [
        jnp.sum(jnp.where(mine & (rank == i), local, 0), axis=-1, dtype=jnp.int32)
        for i in range(cap)
    ]
    count = jnp.sum(mine, axis=-1, dtype=jnp.int32)
    return count.reshape(-1), jnp.stack(slots, axis=-1).reshape(-1)


def per_device(
    queries, local_keys, local_values, memory_keys, memory_values, block_ids, mixing_offset_per_head
):
    devices = lax.axis_size("mem")
    me = lax.axis_index("mem")
    chips = devices // 2
    core = me % 2
    q_heads, keys_own, values_own = (
        lax.all_to_all(x, "head", split_axis=1, concat_axis=0, tiled=True)
        for x in (queries, local_keys, local_values)
    )
    tokens = q_heads.shape[0]
    kv = keys_own.shape[1] // HD
    group = q_heads.shape[1] // (kv * HD)
    half_heads = kv * group // 2
    blocks_here = memory_keys.shape[0] // BL
    cap = (2 * TOPK + devices - 1) // devices

    all_ids = lax.all_gather(block_ids, "mem", axis=0, tiled=True)
    all_queries = lax.all_gather(q_heads, "mem", axis=0, tiled=True)
    cnt, slots = block_tables(all_ids, me * blocks_here, blocks_here, cap)

    behind = [(i, i + 1) for i in range(devices - 1)]
    keys_before, values_before = (lax.ppermute(x, "mem", behind) for x in (keys_own, values_own))
    local_out = local_part(
        me.reshape(1).astype(jnp.int32),
        q_heads,
        jnp.concatenate([keys_before, keys_own], axis=0),
        jnp.concatenate([values_before, values_own], axis=0),
        kv,
        group,
    )
    gate = jnp.repeat(jax.nn.sigmoid(mixing_offset_per_head), HD)[None, :]

    def parts_for(which, cnt):
        return memory_parts(
            which.reshape(1).astype(jnp.int32), cnt, slots, all_queries, memory_keys, memory_values,
            chips, tokens, kv, group, cap,
        )

    siblings = [(i, i ^ 1) for i in range(devices)]
    sib = lax.ppermute(parts_for(1 - core, cnt), "mem", siblings)
    if kv == 1:
        sib, cnt = lax.optimization_barrier((sib, cnt))
    own = parts_for(core, cnt)

    ring = chip_ring(chips)
    order = jnp.array(ring, jnp.int32)
    position = jnp.array([ring.index(c) for c in range(chips)], jnp.int32)[me // 2]
    onward = [
        (ring[i] * 2 + c, ring[(i + 1) % chips] * 2 + c) for i in range(chips) for c in range(2)
    ]
    backward = [(b, a) for a, b in onward]

    received = None
    for step in range(1, chips + 1):
        places = jnp.stack([order[(position - step) % chips], order[(position + step) % chips]])
        if step == chips:
            break
        right, left = merge_step(places, own, sib, received, half_heads)
        received = (
            lax.ppermute(right, "mem", onward),
            lax.ppermute(left, "mem", backward),
        )
    blended = merge_step(places, own, sib, received, half_heads, local_out, gate)
    return lax.all_to_all(blended, "head", split_axis=0, concat_axis=1, tiled=True)


def solution(mesh):
    return jax.shard_map(
        per_device,
        mesh=mesh,
        in_specs=(
            P(("mem", "head"), None),
            P(("mem", "head"), None),
            P(("mem", "head"), None),
            P("mem", "head"),
            P("mem", "head"),
            P("mem", "head", None),
            P("head"),
        ),
        out_specs=P(("mem", "head"), None),
        check_vma=False,
    )
```

time: 631 us -> 485 us (0.77)
  waiting for transfers between devices: 349 us -> 179 us
  Pallas kernels: 0 us -> 169 us
  local copies, waits for them, and re-layouts: 136 us -> 13.2 us
  matrix products: 48.2 us -> 0 us
  blocking collectives: 12.4 us -> 51.1 us
  loops' own time: 28.1 us -> 0 us
  between operations: 0.18 us -> 23.8 us
  starting transfers between devices: 33.7 us -> 25.4 us
    pallas_call x0 -> x11, Pallas kernels: none -> 169 us  [the longest x2 110 us: memory_parts(): pl.pallas_call(functools.partial(part_kernel, group, half_heads, tokens /...]
    all_to_all x6 -> x2, waiting for transfers between devices: 168 us -> 5.82 us  [per_device(): lax.all_to_all(x, 'head', split_axis=1, concat_axis=0, tiled=True)]
    ppermute x2 -> x17, waiting for transfers between devices: 181 us -> 66.7 us  [the longest x7 56.8 us: per_device(): lax.ppermute(right, 'mem', onward)]
    all_gather x0 -> x1, waiting for transfers between devices: none -> 107 us  [per_device(): all_queries = lax.all_gather(q_heads, 'mem', axis=0, tiled=True)]
    gather x21 -> x0, local copies, waits for them, and re-layouts: 92.9 us -> none  [the longest x8 33 us: memory_pair(): value_rows = jnp.take(flat_values, chosen, axis=0).reshape(-1, HD)]
    dot_general x32 -> x0, matrix products: 48.2 us -> none  [the longest x16 26.8 us: attend_block(): jnp.einsum('tgk,kd->tgd', weights.astype(jnp.bfloat16), value_rows, prefe...]
    another operation x1 -> x0, loops' own time: 28.1 us -> none  [per_device(): blended = lax.map(both_parts, pair_list)]
    reshape x9 -> x2, local copies, waits for them, and re-layouts: 27.5 us -> 1.3 us  [block_tables(): return (count.reshape(-1), jnp.stack(slots, axis=-1).reshape(-1))]
  transfers between devices with their start and end apart: 8 -> 20, of which waited for: 6 -> 15; matrix products, arithmetic and copies ran while one was open for 9% -> 5% of each run, Pallas kernels for 0% -> 14%
where the time goes in v1:
time: 485 us; the launch traced here: 479 us
  waiting for transfers between devices  179 us (37%)
  Pallas kernels  169 us (35%)
  blocking collectives  51.1 us (11%)
  starting transfers between devices  25.4 us (5%)
  between operations  23.8 us (5%)
  other arithmetic  18 us (4%)
  local copies, waits for them, and re-layouts  13.2 us (3%)
    pallas_call x2, Pallas kernels, memory_parts(): pl.pallas_call(functools.partial(part_kernel, group, half_heads, tokens /...  110 us
    all_gather x1, waiting for transfers between devices, per_device(): all_queries = lax.all_gather(q_heads, 'mem', axis=0, tiled=True)  107 us
    ppermute x7, waiting for transfers between devices, per_device(): lax.ppermute(right, 'mem', onward)  56.8 us
    pallas_call x8, Pallas kernels, merge_step(): pl.pallas_call(kernel, out_shape=out_shape, grid_spec=pltpu.PrefetchScala...  53 us
    all_to_all x1, blocking collectives, per_device(): lax.all_to_all(blended, 'head', split_axis=0, concat_axis=1, tiled=True)  17.1 us
    all_to_all x1, blocking collectives, per_device(): lax.all_to_all(x, 'head', split_axis=1, concat_axis=0, tiled=True)  17.1 us
    all_gather x1, blocking collectives, per_device(): all_ids = lax.all_gather(block_ids, 'mem', axis=0, tiled=True)  16.9 us
    another operation x8, other arithmetic, per_device(): jnp.stack([order[(position - step) % chips], order[(position + step) % ch...  15.1 us
  transfers between devices with their start and end apart: 20, of which 15 were waited for; matrix products, arithmetic and copies ran while one was open for 5% of the time, Pallas kernels for 14%

profile of v1, /device:TPU:16, one launch (start us, length us, event | category | flops | bytes accessed | tf_op | source)
XLA Modules:
  0.0 479.4 jit_solution(3222995922547559102)
XLA Ops:
  7.8 17.1 %all_to_all.76 = bf16[128,2,2048]{2,0,1:T(8,128)(2,1)} all-to-all(bf16[128,2,2048]{2,0,1:T(8,128)(2,1)S(1)} %bitcast.53), channel_id=1, replica_groups=mesh['mem'=16,'head'=2] {'head'}, dimensions={1} | all-to-all | bytes 2097152 | tf_op jit(solution)/shard_map/all_to_all | solution.py:294
  24.9 16.9 %all_gather.6 = s32[32,4,32]{2,1,0:T(4,128)S(1)} all-gather(s32[2,4,32]{2,1,0:T(4,128)} %param.14), channel_id=1, replica_groups=mesh['mem'=16,'head'=2] {'mem'}, dimensions={0}, use_global_device_ids=true | all-gather | bytes 17408 | tf_op jit(solution)/shard_map/all_gather | solution.py:304
  44.6 106.6 %all-gather.2.cloned.1.call-done.q_ref = bf16[4096,2048]{1,0:T(8,128)(2,1)} async-done(((bf16[256,2048]{1,0:T(8,128)(2,1)}), bf16[4096,2048]{1,0:T(8,128)(2,1)}) %all-gather.2.cloned.1.call-update) | async-done | bytes 16777232 | tf_op jit(solution)/shard_map/all_gather | solution.py:305
  151.2 55.4 %memory_parts.3 = bf16[8,256,2304]{2,1,0:T(8,128)(2,1)} custom-call(s32[1]{0:T(128)} %bitcast.9.sel, s32[128]{0:T(128)} %reshape.60.cnt, s32[512]{0:T(512)} %reshape.61.slots, bf16[4096,2048]{1,0:T(8,128)(2,1)} %all-gather.2.cloned.1.call-done.q_ref, bf16[4096,512]{1,0:T(8,128)(2,1)} %k_ref.3, bf16[4096,512]{1,0:T(8,128)(2,1)} %v_ref.3), custom_call_target="tpu_custom_call" | custom-call | flops 6442450944 | bytes 18874368 | tf_op jit(solution)/shard_map/memory_parts/pallas_call | solution.py:105
  220.2 54.2 %memory_parts.2.refs_0_.refs_1_ = bf16[8,256,2304]{2,1,0:T(8,128)(2,1)} custom-call(s32[1]{0:T(128)} %bitcast.2.sel, s32[128]{0:T(128)} %reshape.60.cnt, s32[512]{0:T(512)} %reshape.61.slots, bf16[4096,2048]{1,0:T(8,128)(2,1)} %all-gather.2.cloned.1.call-done.q_ref, bf16[4096,512]{1,0:T(8,128)(2,1)} %k_ref.3, bf16[4096,512]{1,0:T(8,128)(2,1)} %v_ref.3), custom_call_target="tpu_custom_call" | custom-call | flops 6442450944 | bytes 18874368 | tf_op jit(solution)/shard_map/memory_parts/pallas_call | solution.py:105
  274.4 5.8 %merge_step.7 = (bf16[256,1152]{1,0:T(8,128)(2,1)}, bf16[256,1152]{1,0:T(8,128)(2,1)}) custom-call(s32[2]{0:T(128)} %pad_add_fusion.8.places, bf16[8,256,2304]{2,1,0:T(8,128)(2,1)} %memory_parts.2.refs_0_.refs_1_, bf16[8,256,2304]{2,1,0:T(8,128)(2,1)} %memory_parts.2.refs_0_.refs_1_, bf16[8,256,2304]{2,1,0:T(8,128)(2,1)} %collective-permute-done.refs_2_.refs_3_, ...), custom_call_target="tpu_custom_call" | custom-call | tf_op jit(solution)/shard_map/merge_step/pallas_call | solution.py:251
  280.2 2.0 collective-permute-start.2
  282.3 1.9 pad_add_fusion.7.places
  284.2 9.6 %collective-permute-done.1.refs_4_ = bf16[256,1152]{1,0:T(8,128)(2,1)S(1)} collective-permute-done((bf16[256,1152]{1,0:T(8,128)(2,1)}, bf16[256,1152]{1,0:T(8,128)(2,1)S(1)}, u32[]{:S(2)}, u32[]{:S(2)}) %collective-permute-start.1) | collective-permute-done | bytes 589856 | tf_op jit(solution)/shard_map/ppermute | solution.py:347
  293.8 3.5 collective-permute-done.2.refs_5_
  298.1 6.7 %merge_step.8 = (bf16[256,1152]{1,0:T(8,128)(2,1)}, bf16[256,1152]{1,0:T(8,128)(2,1)}) custom-call(s32[2]{0:T(128)} %pad_add_fusion.7.places, bf16[8,256,2304]{2,1,0:T(8,128)(2,1)} %memory_parts.2.refs_0_.refs_1_, bf16[8,256,2304]{2,1,0:T(8,128)(2,1)} %memory_parts.2.refs_0_.refs_1_, bf16[8,256,2304]{2,1,0:T(8,128)(2,1)} %collective-permute-done.refs_2_.refs_3_, ...), custom_call_target="tpu_custom_call" | custom-call | tf_op jit(solution)/shard_map/merge_step/pallas_call | solution.py:251
  304.8 2.3 collective-permute-start.3
  307.1 1.9 pad_add_fusion.6.places
  309.1 12.0 %collective-permute-done.3.refs_4_ = bf16[256,1152]{1,0:T(8,128)(2,1)S(1)} collective-permute-done((bf16[256,1152]{1,0:T(8,128)(2,1)}, bf16[256,1152]{1,0:T(8,128)(2,1)S(1)}, u32[]{:S(2)}, u32[]{:S(2)}) %collective-permute-start.3) | collective-permute-done | bytes 589856 | tf_op jit(solution)/shard_map/ppermute | solution.py:347
  321.1 2.1 collective-permute-done.4.refs_5_
  324.0 6.7 %merge_step.9 = (bf16[256,1152]{1,0:T(8,128)(2,1)}, bf16[256,1152]{1,0:T(8,128)(2,1)}) custom-call(s32[2]{0:T(128)} %pad_add_fusion.6.places, bf16[8,256,2304]{2,1,0:T(8,128)(2,1)} %memory_parts.2.refs_0_.refs_1_, bf16[8,256,2304]{2,1,0:T(8,128)(2,1)} %memory_parts.2.refs_0_.refs_1_, bf16[8,256,2304]{2,1,0:T(8,128)(2,1)} %collective-permute-done.refs_2_.refs_3_, ...), custom_call_target="tpu_custom_call" | custom-call | tf_op jit(solution)/shard_map/merge_step/pallas_call | solution.py:251
  334.5 11.4 %collective-permute-done.5.refs_4_ = bf16[256,1152]{1,0:T(8,128)(2,1)S(1)} collective-permute-done((bf16[256,1152]{1,0:T(8,128)(2,1)}, bf16[256,1152]{1,0:T(8,128)(2,1)S(1)}, u32[]{:S(2)}, u32[]{:S(2)}) %collective-permute-start.5) | collective-permute-done | bytes 589856 | tf_op jit(solution)/shard_map/ppermute | solution.py:347
  347.7 6.7 %merge_step.10 = (bf16[256,1152]{1,0:T(8,128)(2,1)}, bf16[256,1152]{1,0:T(8,128)(2,1)}) custom-call(s32[2]{0:T(128)} %pad_add_fusion.5.places, bf16[8,256,2304]{2,1,0:T(8,128)(2,1)} %memory_parts.2.refs_0_.refs_1_, bf16[8,256,2304]{2,1,0:T(8,128)(2,1)} %memory_parts.2.refs_0_.refs_1_, bf16[8,256,2304]{2,1,0:T(8,128)(2,1)} %collective-permute-done.refs_2_.refs_3_, ...), custom_call_target="tpu_custom_call" | custom-call | tf_op jit(solution)/shard_map/merge_step/pallas_call | solution.py:251
  358.3 10.4 %collective-permute-done.7.refs_4_ = bf16[256,1152]{1,0:T(8,128)(2,1)S(1)} collective-permute-done((bf16[256,1152]{1,0:T(8,128)(2,1)}, bf16[256,1152]{1,0:T(8,128)(2,1)S(1)}, u32[]{:S(2)}, u32[]{:S(2)}) %collective-permute-start.7) | collective-permute-done | bytes 589856 | tf_op jit(solution)/shard_map/ppermute | solution.py:347
  370.7 6.7 %merge_step.11 = (bf16[256,1152]{1,0:T(8,128)(2,1)}, bf16[256,1152]{1,0:T(8,128)(2,1)}) custom-call(s32[2]{0:T(128)} %pad_add_fusion.4.places, bf16[8,256,2304]{2,1,0:T(8,128)(2,1)} %memory_parts.2.refs_0_.refs_1_, bf16[8,256,2304]{2,1,0:T(8,128)(2,1)} %memory_parts.2.refs_0_.refs_1_, bf16[8,256,2304]{2,1,0:T(8,128)(2,1)} %collective-permute-done.refs_2_.refs_3_, ...), custom_call_target="tpu_custom_call" | custom-call | tf_op jit(solution)/shard_map/merge_step/pallas_call | solution.py:251
  381.3 9.4 %collective-permute-done.9.refs_4_ = bf16[256,1152]{1,0:T(8,128)(2,1)S(1)} collective-permute-done((bf16[256,1152]{1,0:T(8,128)(2,1)}, bf16[256,1152]{1,0:T(8,128)(2,1)S(1)}, u32[]{:S(2)}, u32[]{:S(2)}) %collective-permute-start.9) | collective-permute-done | bytes 589856 | tf_op jit(solution)/shard_map/ppermute | solution.py:347
  392.6 6.7 %merge_step.12 = (bf16[256,1152]{1,0:T(8,128)(2,1)}, bf16[256,1152]{1,0:T(8,128)(2,1)}) custom-call(s32[2]{0:T(128)} %pad_add_fusion.3.places, bf16[8,256,2304]{2,1,0:T(8,128)(2,1)} %memory_parts.2.refs_0_.refs_1_, bf16[8,256,2304]{2,1,0:T(8,128)(2,1)} %memory_parts.2.refs_0_.refs_1_, bf16[8,256,2304]{2,1,0:T(8,128)(2,1)} %collective-permute-done.refs_2_.refs_3_, ...), custom_call_target="tpu_custom_call" | custom-call | tf_op jit(solution)/shard_map/merge_step/pallas_call | solution.py:251
  402.1 3.4 all-to-all-start.1
  406.3 4.4 all-to-all-done.1
  410.7 3.4 all-to-all-start.2
  419.3 2.0 collective-permute-start.16
  423.0 6.7 %merge_step.13 = (bf16[256,1152]{1,0:T(8,128)(2,1)}, bf16[256,1152]{1,0:T(8,128)(2,1)}) custom-call(s32[2]{0:T(128)} %pad_add_fusion.2.places, bf16[8,256,2304]{2,1,0:T(8,128)(2,1)} %memory_parts.2.refs_0_.refs_1_, bf16[8,256,2304]{2,1,0:T(8,128)(2,1)} %memory_parts.2.refs_0_.refs_1_, bf16[8,256,2304]{2,1,0:T(8,128)(2,1)} %collective-permute-done.refs_2_.refs_3_, ...), custom_call_target="tpu_custom_call" | custom-call | tf_op jit(solution)/shard_map/merge_step/pallas_call | solution.py:251
  431.7 1.9 pad_add_fusion.1.places
  435.3 6.2 %local_part.1.refs_6_ = f32[256,2048]{1,0:T(8,128)} custom-call(s32[1]{0:T(128)} %bitcast.24.me, bf16[256,2048]{1,0:T(8,128)(2,1)} %bitcast.51, bf16[512,512]{1,0:T(8,128)(2,1)} %pad_maximum_fusion.k_ref, bf16[512,512]{1,0:T(8,128)(2,1)} %pad_maximum_fusion.1.v_ref), custom_call_target="tpu_custom_call" | custom-call | flops 1207959552 | bytes 3145728 | tf_op jit(solution)/shard_map/local_part/pallas_call | solution.py:146
  441.5 3.9 collective-permute-done.13.refs_4_
  447.4 7.1 %merge_last.1 = bf16[256,2048]{1,0:T(8,128)(2,1)} custom-call(s32[2]{0:T(128)} %pad_add_fusion.1.places, bf16[8,256,2304]{2,1,0:T(8,128)(2,1)} %memory_parts.2.refs_0_.refs_1_, bf16[8,256,2304]{2,1,0:T(8,128)(2,1)} %memory_parts.2.refs_0_.refs_1_, bf16[8,256,2304]{2,1,0:T(8,128)(2,1)} %collective-permute-done.refs_2_.refs_3_, ...), custom_call_target="tpu_custom_call" | custom-call | tf_op jit(solution)/shard_map/merge_last/pallas_call | solution.py:251
  454.4 17.1 %all_to_all.77 = bf16[2,128,2048]{2,1,0:T(8,128)(2,1)S(1)} all-to-all(bf16[2,128,2048]{2,1,0:T(8,128)(2,1)} %bitcast.49), channel_id=1, replica_groups=mesh['mem'=16,'head'=2] {'head'}, dimensions={0} | all-to-all | bytes 2097152 | tf_op jit(solution)/shard_map/all_to_all | solution.py:351
  (87 shorter events, 43.3 us)
Async XLA Ops:
  6.5 144.7 %all-gather.2.cloned.1.call-start = ((), (), s32[]{:S(2)}) async-start(), calls=%async_computation.4 | async-start | bytes 17825792 | tf_op jit(solution)/shard_map/all_gather | solution.py:305
  151.2 55.5 %copy-start.18 = (s32[8]{0:T(128)S(1)}, s32[8]{0:T(128)}, u32[]{:S(2)}) copy-start(s32[8]{0:T(128)} %constant.166.clone) | copy-start | bytes 100
  151.2 66.3 %copy-start.16 = (s32[8]{0:T(128)S(1)}, s32[8]{0:T(128)}, u32[]{:S(2)}) copy-start(s32[8]{0:T(128)} %constant.165.clone) | copy-start | bytes 100
  206.6 67.8 %collective-permute-start = (bf16[8,256,2304]{2,1,0:T(8,128)(2,1)}, bf16[8,256,2304]{2,1,0:T(8,128)(2,1)}, u32[]{:S(2)}, u32[]{:S(2)}) collective-permute-start(bf16[8,256,2304]{2,1,0:T(8,128)(2,1)} %memory_parts.3), channel_id=1, source_target_pairs={{0,2},{2,0},{4,6},{6,4},{8,10},{10,8},{12,14},{14,12},{16,18},{18,... | collective-permute-start | bytes 28311560 | tf_op jit(solution)/shard_map/ppermute | solution.py:327
  280.2 13.6 %collective-permute-start.1 = (bf16[256,1152]{1,0:T(8,128)(2,1)}, bf16[256,1152]{1,0:T(8,128)(2,1)S(1)}, u32[]{:S(2)}, u32[]{:S(2)}) collective-permute-start(bf16[256,1152]{1,0:T(8,128)(2,1)} %get-tuple-element.19), channel_id=1, source_target_pairs={{4,12},{6,14},{12,20},{14,22},{20,28},{22,30},{28,24},{30,26},{24,... | collective-permute-start | bytes 1769480 | tf_op jit(solution)/shard_map/ppermute | solution.py:347
  280.2 17.0 %collective-permute-start.2 = (bf16[256,1152]{1,0:T(8,128)(2,1)}, bf16[256,1152]{1,0:T(8,128)(2,1)S(1)}, u32[]{:S(2)}, u32[]{:S(2)}) collective-permute-start(bf16[256,1152]{1,0:T(8,128)(2,1)} %get-tuple-element.20), channel_id=1, source_target_pairs={{12,4},{14,6},{20,12},{22,14},{28,20},{30,22},{24,28},{26,30},{16,... | collective-permute-start | bytes 1769480 | tf_op jit(solution)/shard_map/ppermute | solution.py:348
  293.8 3.5 copy-start.4
  304.8 16.3 %collective-permute-start.3 = (bf16[256,1152]{1,0:T(8,128)(2,1)}, bf16[256,1152]{1,0:T(8,128)(2,1)S(1)}, u32[]{:S(2)}, u32[]{:S(2)}) collective-permute-start(bf16[256,1152]{1,0:T(8,128)(2,1)} %get-tuple-element.21), channel_id=1, source_target_pairs={{4,12},{6,14},{12,20},{14,22},{20,28},{22,30},{28,24},{30,26},{24,... | collective-permute-start | bytes 1769480 | tf_op jit(solution)/shard_map/ppermute | solution.py:347
  307.1 16.0 %collective-permute-start.4 = (bf16[256,1152]{1,0:T(8,128)(2,1)}, bf16[256,1152]{1,0:T(8,128)(2,1)S(1)}, u32[]{:S(2)}, u32[]{:S(2)}) collective-permute-start(bf16[256,1152]{1,0:T(8,128)(2,1)} %get-tuple-element.22), channel_id=1, source_target_pairs={{12,4},{14,6},{20,12},{22,14},{28,20},{30,22},{24,28},{26,30},{16,... | collective-permute-start | bytes 1769480 | tf_op jit(solution)/shard_map/ppermute | solution.py:348
  321.1 2.1 copy-start.5
  330.7 15.2 %collective-permute-start.5 = (bf16[256,1152]{1,0:T(8,128)(2,1)}, bf16[256,1152]{1,0:T(8,128)(2,1)S(1)}, u32[]{:S(2)}, u32[]{:S(2)}) collective-permute-start(bf16[256,1152]{1,0:T(8,128)(2,1)} %get-tuple-element.23), channel_id=1, source_target_pairs={{4,12},{6,14},{12,20},{14,22},{20,28},{22,30},{28,24},{30,26},{24,... | collective-permute-start | bytes 1769480 | tf_op jit(solution)/shard_map/ppermute | solution.py:347
  331.8 15.2 %collective-permute-start.6 = (bf16[256,1152]{1,0:T(8,128)(2,1)}, bf16[256,1152]{1,0:T(8,128)(2,1)S(1)}, u32[]{:S(2)}, u32[]{:S(2)}) collective-permute-start(bf16[256,1152]{1,0:T(8,128)(2,1)} %get-tuple-element.24), channel_id=1, source_target_pairs={{12,4},{14,6},{20,12},{22,14},{28,20},{30,22},{24,28},{26,30},{16,... | collective-permute-start | bytes 1769480 | tf_op jit(solution)/shard_map/ppermute | solution.py:348
  345.9 1.0 copy-start.6
  354.4 14.3 %collective-permute-start.7 = (bf16[256,1152]{1,0:T(8,128)(2,1)}, bf16[256,1152]{1,0:T(8,128)(2,1)S(1)}, u32[]{:S(2)}, u32[]{:S(2)}) collective-permute-start(bf16[256,1152]{1,0:T(8,128)(2,1)} %get-tuple-element.25), channel_id=1, source_target_pairs={{4,12},{6,14},{12,20},{14,22},{20,28},{22,30},{28,24},{30,26},{24,... | collective-permute-start | bytes 1769480 | tf_op jit(solution)/shard_map/ppermute | solution.py:347
  355.5 14.3 %collective-permute-start.8 = (bf16[256,1152]{1,0:T(8,128)(2,1)}, bf16[256,1152]{1,0:T(8,128)(2,1)S(1)}, u32[]{:S(2)}, u32[]{:S(2)}) collective-permute-start(bf16[256,1152]{1,0:T(8,128)(2,1)} %get-tuple-element.26), channel_id=1, source_target_pairs={{12,4},{14,6},{20,12},{22,14},{28,20},{30,22},{24,28},{26,30},{16,... | collective-permute-start | bytes 1769480 | tf_op jit(solution)/shard_map/ppermute | solution.py:348
  368.7 1.1 copy-start.7
  377.3 13.4 %collective-permute-start.9 = (bf16[256,1152]{1,0:T(8,128)(2,1)}, bf16[256,1152]{1,0:T(8,128)(2,1)S(1)}, u32[]{:S(2)}, u32[]{:S(2)}) collective-permute-start(bf16[256,1152]{1,0:T(8,128)(2,1)} %get-tuple-element.27), channel_id=1, source_target_pairs={{4,12},{6,14},{12,20},{14,22},{20,28},{22,30},{28,24},{30,26},{24,... | collective-permute-start | bytes 1769480 | tf_op jit(solution)/shard_map/ppermute | solution.py:347
  378.4 13.4 %collective-permute-start.10 = (bf16[256,1152]{1,0:T(8,128)(2,1)}, bf16[256,1152]{1,0:T(8,128)(2,1)S(1)}, u32[]{:S(2)}, u32[]{:S(2)}) collective-permute-start(bf16[256,1152]{1,0:T(8,128)(2,1)} %get-tuple-element.28), channel_id=1, source_target_pairs={{12,4},{14,6},{20,12},{22,14},{28,20},{30,22},{24,28},{26,30},{16,... | collective-permute-start | bytes 1769480 | tf_op jit(solution)/shard_map/ppermute | solution.py:348
  381.3 20.1 %copy-start.14 = (bf16[128,1024]{1,0:T(8,128)(2,1)S(1)}, bf16[128,1024]{1,0:T(8,128)(2,1)}, u32[]{:S(2)}) copy-start(bf16[128,1024]{1,0:T(8,128)(2,1)} %param.10) | copy-start | bytes 786436
  381.3 24.3 %copy-start.15 = (bf16[128,1024]{1,0:T(8,128)(2,1)S(1)}, bf16[128,1024]{1,0:T(8,128)(2,1)}, u32[]{:S(2)}) copy-start(bf16[128,1024]{1,0:T(8,128)(2,1)} %param.11) | copy-start | bytes 786436
  390.7 1.1 copy-start.8
  399.3 22.0 %collective-permute-start.11 = (bf16[256,1152]{1,0:T(8,128)(2,1)}, bf16[256,1152]{1,0:T(8,128)(2,1)S(1)}, u32[]{:S(2)}, u32[]{:S(2)}) collective-permute-start(bf16[256,1152]{1,0:T(8,128)(2,1)} %get-tuple-element.29), channel_id=1, source_target_pairs={{4,12},{6,14},{12,20},{14,22},{20,28},{22,30},{28,24},{30,26},{24,... | collective-permute-start | bytes 1769480 | tf_op jit(solution)/shard_map/ppermute | solution.py:347
  400.4 21.0 %collective-permute-start.12 = (bf16[256,1152]{1,0:T(8,128)(2,1)}, bf16[256,1152]{1,0:T(8,128)(2,1)S(1)}, u32[]{:S(2)}, u32[]{:S(2)}) collective-permute-start(bf16[256,1152]{1,0:T(8,128)(2,1)} %get-tuple-element.30), channel_id=1, source_target_pairs={{12,4},{14,6},{20,12},{22,14},{28,20},{30,22},{24,28},{26,30},{16,... | collective-permute-start | bytes 1769480 | tf_op jit(solution)/shard_map/ppermute | solution.py:348
  402.1 8.6 %all-to-all-start.1 = ((bf16[128,2,512]{2,0,1:T(8,128)(2,1)}), bf16[128,2,512]{2,0,1:T(8,128)(2,1)S(1)}, u32[]{:S(2)}, u32[]{:S(2)}) async-start(bf16[128,2,512]{2,0,1:T(8,128)(2,1)} %bitcast.48), calls=%async_computation.1 | async-start | bytes 524288 | tf_op jit(solution)/shard_map/all_to_all | solution.py:294
  410.7 8.6 %all-to-all-start.2 = ((bf16[128,2,512]{2,0,1:T(8,128)(2,1)}), bf16[128,2,512]{2,0,1:T(8,128)(2,1)S(1)}, u32[]{:S(2)}, u32[]{:S(2)}) async-start(bf16[128,2,512]{2,0,1:T(8,128)(2,1)} %bitcast.47), calls=%async_computation.2 | async-start | bytes 524288 | tf_op jit(solution)/shard_map/all_to_all | solution.py:294
  416.0 17.6 %collective-permute-start.15 = (bf16[256,512]{1,0:T(8,128)(2,1)S(1)}, bf16[256,512]{1,0:T(8,128)(2,1)S(1)}, u32[]{:S(2)}, u32[]{:S(2)}) collective-permute-start(bf16[256,512]{1,0:T(8,128)(2,1)S(1)} %bitcast.55), channel_id=1, source_target_pairs={{0,2},{2,4},{4,6},{6,8},{8,10},{10,12},{12,14},{14,16},{16,18},{18... | collective-permute-start | bytes 786440 | tf_op jit(solution)/shard_map/ppermute | solution.py:309
  419.3 12.4 %copy-start.17 = (f32[16]{0:T(128)S(1)}, f32[16]{0:T(128)}, u32[]{:S(2)}) copy-start(f32[16]{0:T(128)} %param.15) | copy-start | bytes 196
  419.3 15.2 %collective-permute-start.16 = (bf16[256,512]{1,0:T(8,128)(2,1)S(1)}, bf16[256,512]{1,0:T(8,128)(2,1)S(1)}, u32[]{:S(2)}, u32[]{:S(2)}) collective-permute-start(bf16[256,512]{1,0:T(8,128)(2,1)S(1)} %bitcast.57), channel_id=1, source_target_pairs={{0,2},{2,4},{4,6},{6,8},{8,10},{10,12},{12,14},{14,16},{16,18},{18... | collective-permute-start | bytes 786440 | tf_op jit(solution)/shard_map/ppermute | solution.py:309
  429.7 15.7 %collective-permute-start.13 = (bf16[256,1152]{1,0:T(8,128)(2,1)}, bf16[256,1152]{1,0:T(8,128)(2,1)S(1)}, u32[]{:S(2)}, u32[]{:S(2)}) collective-permute-start(bf16[256,1152]{1,0:T(8,128)(2,1)} %get-tuple-element.31), channel_id=1, source_target_pairs={{4,12},{6,14},{12,20},{14,22},{20,28},{22,30},{28,24},{30,26},{24,... | collective-permute-start | bytes 1769480 | tf_op jit(solution)/shard_map/ppermute | solution.py:347
  430.8 15.8 %collective-permute-start.14 = (bf16[256,1152]{1,0:T(8,128)(2,1)}, bf16[256,1152]{1,0:T(8,128)(2,1)S(1)}, u32[]{:S(2)}, u32[]{:S(2)}) collective-permute-start(bf16[256,1152]{1,0:T(8,128)(2,1)} %get-tuple-element.32), channel_id=1, source_target_pairs={{12,4},{14,6},{20,12},{22,14},{28,20},{30,22},{24,28},{26,30},{16,... | collective-permute-start | bytes 1769480 | tf_op jit(solution)/shard_map/ppermute | solution.py:348
  445.4 1.9 copy-start.2
  446.5 0.8 copy-start.3
  (7 other events, 5.7 us)
Sparse Core Ops, SparseCore 0:
  25.1 126.1 all-gather.1
